TPU v7x, 32 devices: a whole 2x2x4 slice. The times are simulated.
32 devices in a mesh: groups: 2 (over y), tp: 4 (over z), ad: 2 (over x), rep: 2 (over core).
Axes of the slice: x: 2, y: 2, z: 4, core: 2. Of those that a mesh axis runs over, the one named last changes fastest.
Arguments:
- tokens: bfloat16 [4096, 8192], P(('groups', 'ad', 'rep'), 'tp'), parts along dimension 0, may hold values from -6 to 6
- adapter_per_block: int32 [32], P(('groups', 'ad', 'rep')), parts along dimension 0, may hold values from 0 to 31, as said below
- placement: int32 [32], replicated, may hold values from 0 to 31, as said below
- weight: bfloat16 [8192, 4096], P('rep', 'tp'), may hold values from -0.0625 to 0.0625
- lowrank_down_weight: bfloat16 [32, 64, 8192], P('ad', None, 'tp'), may hold values from -0.0625 to 0.0625
- lowrank_up_weight: bfloat16 [32, 64, 4096], P('ad', None, 'tp'), may hold values from -0.75 to 0.75
Outputs:
- queries: bfloat16 [4096, 4096], P(('groups', 'ad', 'rep'), 'tp'), parts along dimension 0
There are 2 independent parts, one for each index of `groups`. A program takes and returns all parts, laid end to end along the dimension named above; an argument that names none is the same for every part. Nothing has to cross between parts.
Inputs may be any that keep to these rules, and one draw needn't show every extreme that they name: Store row placement[a] lies on store shard a mod (2), shard k holding rows k * 16 to (k + 1) * 16 - 1; every store row is named once. `adapter_per_block`: of the 4 blocks of one device, at most 2 name adapters stored on one store shard, and in every draw some shard is named by exactly 2 blocks of some device. Adapters 0 and 31 are named in every draw.
All inputs are finite; a program needn't handle non-finite values.
Results may differ from a plain program's by a relative error of at most 0.0046.
Values may be sent and summed in bfloat16 or wider, within the bound.
A program may use at most 128 MiB of HBM per device.

v0:
```python
import jax
import jax.numpy as jnp
from jax import lax
from jax.sharding import PartitionSpec as P

lowrank_scale = 2.0


def partner(array, axis, apart):
    return lax.ppermute(array, axis, [(i, i ^ 1 << apart) for i in range(lax.axis_size(axis))])


def body(tokens, adapter_per_block, placement, weight, lowrank_down_weight, lowrank_up_weight):
    count_of_rows = tokens.shape[0]
    feat_local = tokens.shape[1]
    block_count = adapter_per_block.shape[0]
    block_size = count_of_rows // block_count
    count_of_slots = lowrank_down_weight.shape[0]
    rank_width = lowrank_down_weight.shape[1]
    column_count = weight.shape[1]
    half_rows = weight.shape[0]
    owner_count = lax.axis_size("ad")
    table = jnp.arange(placement.shape[0], dtype=jnp.int32)
    store_row_index = jnp.sum(
        jnp.where(adapter_per_block[:, None] == table[None, :], placement[None, :], 0), axis=1
    )
    owner_of = store_row_index // count_of_slots
    slot_of = store_row_index % count_of_slots
    per_owner = (block_count + owner_count - 1) // owner_count
    block_index = jnp.arange(block_count, dtype=jnp.int32)
    earlier_same = (owner_of[:, None] == owner_of[None, :]) & (
        block_index[None, :] < block_index[:, None]
    )
    order_in = jnp.sum(earlier_same.astype(jnp.int32), axis=1)
    position = owner_of * per_owner + order_in
    slot_table = jnp.arange(owner_count * per_owner, dtype=jnp.int32)
    flat_requests = (
        jnp.sum(
            jnp.where(position[None, :] == slot_table[:, None], slot_of[None, :] + 1, 0), axis=1
        )
        - 1
    )
    requests = flat_requests.reshape(owner_count, per_owner)
    asked_slots = lax.all_to_all(requests, "ad", split_axis=0, concat_axis=0, tiled=True)
    valid_mask = asked_slots >= 0
    clamped_index = jnp.clip(asked_slots, 0, count_of_slots - 1)
    down_pick = jnp.where(
        valid_mask[..., None, None],
        jnp.take(lowrank_down_weight, clamped_index, axis=0),
        jnp.zeros((), jnp.bfloat16),
    )
    up_pick = jnp.where(
        valid_mask[..., None, None],
        jnp.take(lowrank_up_weight, clamped_index, axis=0),
        jnp.zeros((), jnp.bfloat16),
    )
    down_back = lax.all_to_all(down_pick, "ad", split_axis=0, concat_axis=0, tiled=True)
    up_back = lax.all_to_all(up_pick, "ad", split_axis=0, concat_axis=0, tiled=True)
    down_flat = down_back.reshape(owner_count * per_owner, rank_width, feat_local)
    up_flat = up_back.reshape(owner_count * per_owner, rank_width, column_count)
    adapter_down = jnp.take(down_flat, position, axis=0)
    adapter_up_weight = jnp.take(up_flat, position, axis=0)
    gathered = lax.all_gather(tokens, "tp", axis=1, tiled=True)
    core_index = lax.axis_index("rep")
    own_part = lax.dynamic_slice_in_dim(gathered, core_index * half_rows, half_rows, 1)
    lent_part = lax.dynamic_slice_in_dim(gathered, (1 - core_index) * half_rows, half_rows, 1)
    borrowed = partner(lent_part, "rep", 0)
    their_sums = jnp.dot(borrowed, weight, preferred_element_type=jnp.float32)
    returned = partner(their_sums, "rep", 0)
    base_output = jnp.dot(own_part, weight, preferred_element_type=jnp.float32) + returned
    shaped = tokens.reshape(block_count, block_size, feat_local)
    partial_value = jnp.einsum(
        "bnd,brd->bnr", shaped, adapter_down, preferred_element_type=jnp.float32
    )
    summed = lax.psum(partial_value.reshape(block_count, block_size * rank_width), "tp")
    reduced_sum = summed.reshape(block_count, block_size, rank_width).astype(jnp.bfloat16)
    lowrank_output = jnp.einsum(
        "ajw,aws->ajs", reduced_sum, adapter_up_weight, preferred_element_type=jnp.float32
    )
    lowrank_output = lowrank_output.reshape(count_of_rows, column_count)
    return (base_output + lowrank_scale * lowrank_output).astype(jnp.bfloat16)


def solution(mesh):
    return jax.shard_map(
        body,
        mesh=mesh,
        in_specs=(
            P(("groups", "ad", "rep"), "tp"),
            P(("groups", "ad", "rep")),
            P(),
            P("rep", "tp"),
            P("ad", None, "tp"),
            P("ad", None, "tp"),
        ),
        out_specs=P(("groups", "ad", "rep"), "tp"),
        check_vma=False,
    )
```

profile of v0, /device:TPU:0, one launch (start us, length us, event | category | flops | bytes accessed | tf_op | source)
XLA Modules:
  0.0 252.9 jit_solution(9773058493508116873)
XLA Ops:
  6.5 0.0 copy-start
  6.5 0.0 all-gather.2.cloned.1.call-start
  6.5 0.7 all-gather.2.cloned.1.call-update
  7.3 0.0 copy-start.4
  7.3 0.0 copy-start.5
  7.3 154.0 %all-gather.2.cloned.1.call-done = bf16[512,8192]{1,0:T(8,128)(2,1)} async-done(((bf16[512,2048]{1,0:T(8,128)(2,1)}), bf16[512,8192]{1,0:T(8,128)(2,1)}) %all-gather.2.cloned.1.call-update) | async-done | bytes 8388624 | tf_op jit(solution)/shard_map/all_gather | solution.py:63
  161.3 4.6 %constant_dynamic-slice_fusion = bf16[512,4096]{1,0:T(8,128)(2,1)} fusion(bf16[512,8192]{1,0:T(8,128)(2,1)} %all-gather.2.cloned.1.call-done, s32[]{:T(128)S(6)} %select_n.111), kind=kLoop, calls=%fused_computation.50 | loop fusion | bytes 8388612 | tf_op jit(solution)/shard_map/dynamic_slice | solution.py:66
  165.9 0.1 collective-permute-start
  166.0 0.0 copy-done.4
  166.0 0.0 copy-done.5
  166.0 0.2 select_reduce_fusion.1
  166.2 0.2 convert_reduce_fusion
  166.4 0.1 select_reduce_fusion
  166.5 0.1 sub.17
  166.6 6.3 %all_to_all.16 = s32[2,1,2]{2,1,0:T(1,128)S(1)} all-to-all(s32[2,1,2]{2,1,0:T(1,128)S(1)} %bitcast.48), channel_id=1, replica_groups=mesh['groups'=2,'tp'=4,'ad'=2,'rep'=2] {'ad'}, dimensions={0} | all-to-all | bytes 32 | tf_op jit(solution)/shard_map/all_to_all | solution.py:44
  172.9 0.1 reshape.193
  173.0 0.0 copy-done
  173.0 0.6 gather_fusion.2
  173.6 0.9 select_select_fusion.1
  174.5 4.2 %all-to-all-start.2 = ((bf16[2,2,64,1024]{3,2,1,0:T(8,128)(2,1)}), bf16[2,2,64,1024]{3,2,1,0:T(8,128)(2,1)}, u32[]{:S(2)}, u32[]{:S(2)}) async-start(bf16[2,2,64,1024]{3,2,1,0:T(8,128)(2,1)} %select_select_fusion.1), calls=%async_computation.2 | async-start | bytes 1048576 | tf_op jit(solution)/shard_map/all_to_all | solution.py:58
  178.7 2.8 %gather_fusion = bf16[4,64,2048]{2,1,0:T(8,128)(2,1)S(1)} fusion(bf16[16,64,2048]{2,1,0:T(8,128)(2,1)} %param.10, s32[1024]{0:T(1024)S(1)} %pad_clamp_fusion.1), kind=kCustom, calls=%fused_computation | custom fusion | bytes 2097168 | tf_op jit(solution)/shard_map/jit(_take)/gather | solution.py:49
  181.5 1.2 select_select_fusion
  182.7 3.6 %all-to-all-done.2 = bf16[2,2,64,1024]{3,2,1,0:T(8,128)(2,1)} async-done(((bf16[2,2,64,1024]{3,2,1,0:T(8,128)(2,1)}), bf16[2,2,64,1024]{3,2,1,0:T(8,128)(2,1)}, u32[]{:S(2)}, u32[]{:S(2)}) %all-to-all-start.2) | async-done | bytes 524320 | tf_op jit(solution)/shard_map/all_to_all | solution.py:58
  186.3 3.6 %all-to-all-start.1 = ((bf16[2,2,64,2048]{3,2,1,0:T(8,128)(2,1)}), bf16[2,2,64,2048]{3,2,1,0:T(8,128)(2,1)S(1)}, u32[]{:S(2)}, u32[]{:S(2)}) async-start(bf16[2,2,64,2048]{3,2,1,0:T(8,128)(2,1)} %select_select_fusion), calls=%async_computation.1 | async-start | bytes 2097152 | tf_op jit(solution)/shard_map/all_to_all | solution.py:57
  190.0 2.4 gather_fusion.3
  192.4 9.7 %all-to-all-done.1 = bf16[2,2,64,2048]{3,2,1,0:T(8,128)(2,1)S(1)} async-done(((bf16[2,2,64,2048]{3,2,1,0:T(8,128)(2,1)}), bf16[2,2,64,2048]{3,2,1,0:T(8,128)(2,1)S(1)}, u32[]{:S(2)}, u32[]{:S(2)}) %all-to-all-start.1) | async-done | bytes 1048608 | tf_op jit(solution)/shard_map/all_to_all | solution.py:57
  202.1 1.6 gather_fusion.1
  203.7 0.0 copy-start.1
  203.7 0.0 copy-start.3
  203.7 0.0 collective-permute-done
  203.7 10.6 %fusion.15 = f32[512,1024]{1,0:T(8,128)} fusion(bf16[512,4096]{1,0:T(8,128)(2,1)} %collective-permute-done, bf16[4096,1024]{1,0:T(8,128)(2,1)} %param.9), kind=kOutput, calls=%fused_computation.55 | convolution fusion | flops 4294967296 | bytes 14680064 | tf_op jit(solution)/shard_map/dot_general | solution.py:68
  214.3 0.0 copy-start.2
  214.3 0.0 collective-permute-start.1
  214.3 0.0 copy-done.1
  214.3 0.0 copy-done.3
  214.4 0.9 convolution_bitcast_fusion
  215.2 0.1 copy.16
  215.4 0.1 reshape.189
  215.5 18.6 %all-reduce.1 = bf16[4,8192]{1,0:T(4,128)(2,1)S(1)} all-reduce(f32[4,8192]{1,0:T(4,128)S(1)} %reshape.189), channel_id=1, replica_groups=mesh['groups'=2,'tp'=4,'ad'=2,'rep'=2] {'tp'}, use_global_device_ids=true, to_apply=%region_3.4 | all-reduce | flops 32768 | bytes 196608 | tf_op jit(solution)/shard_map/psum | solution.py:75
  234.1 0.2 convert_element_type.14
  234.3 0.0 copy-done.2
  234.3 0.5 convolution_multiply_fusion
  234.8 8.2 %fusion = f32[512,1024]{1,0:T(8,128)S(1)} fusion(bf16[4096,1024]{1,0:T(8,128)(2,1)} %param.9, bf16[512,8192]{1,0:T(8,128)(2,1)} %all-gather.2.cloned.1.call-done, s32[]{:T(128)S(6)} %select_n.110), kind=kOutput, calls=%fused_computation.4 | convolution fusion | flops 4294967296 | bytes 14680068 | tf_op jit(solution)/shard_map/dot_general | solution.py:70
  242.9 0.0 collective-permute-done.1
  242.9 3.1 %fusion.2 = bf16[512,1024]{1,0:T(8,128)(2,1)} fusion(f32[4,128,1024]{2,1,0:T(8,128)S(1)} %convolution_multiply_fusion, f32[512,1024]{1,0:T(8,128)S(1)} %fusion, f32[512,1024]{1,0:T(8,128)} %collective-permute-done.1), kind=kLoop, calls=%fused_computation.7 | loop fusion | flops 1572864 | bytes 7340032 | tf_op jit(solution)/shard_map/convert_element_type | solution.py:81
  (11 shorter events, 0.1 us)
Async XLA Ops:
  6.5 166.5 %copy-start = (bf16[16,64,1024]{2,1,0:T(8,128)(2,1)S(1)}, bf16[16,64,1024]{2,1,0:T(8,128)(2,1)}, u32[]{:S(2)}) copy-start(bf16[16,64,1024]{2,1,0:T(8,128)(2,1)} %param.11) | copy-start | bytes 6291460
  6.5 154.8 %all-gather.2.cloned.1.call-start = ((), (), s32[]{:S(2)}) async-start(), calls=%async_computation.3 | async-start | bytes 10485760 | tf_op jit(solution)/shard_map/all_gather | solution.py:63
  7.3 158.7 %copy-start.4 = (s32[32]{0:T(128)S(1)}, s32[32]{0:T(128)}, u32[]{:S(2)}) copy-start(s32[32]{0:T(128)} %param.8) | copy-start | bytes 388
  7.3 158.7 %copy-start.5 = (s32[4]{0:T(128)S(1)}, s32[4]{0:T(128)}, u32[]{:S(2)}) copy-start(s32[4]{0:T(128)} %param.7) | copy-start | bytes 52
  165.9 37.8 %collective-permute-start = (bf16[512,4096]{1,0:T(8,128)(2,1)}, bf16[512,4096]{1,0:T(8,128)(2,1)}, u32[]{:S(2)}, u32[]{:S(2)}) collective-permute-start(bf16[512,4096]{1,0:T(8,128)(2,1)} %constant_dynamic-slice_fusion), channel_id=1, source_target_pairs={{0,1},{1,0},{2,3},{3,2},{4,5},{5,4},{6,7},{7,6},{8,9},{9,8},{10,11... | collective-permute-start | bytes 12582920 | tf_op jit(solution)/shard_map/ppermute | solution.py:10
  174.5 11.8 %all-to-all-start.2 = ((bf16[2,2,64,1024]{3,2,1,0:T(8,128)(2,1)}), bf16[2,2,64,1024]{3,2,1,0:T(8,128)(2,1)}, u32[]{:S(2)}, u32[]{:S(2)}) async-start(bf16[2,2,64,1024]{3,2,1,0:T(8,128)(2,1)} %select_select_fusion.1), calls=%async_computation.2 | async-start | bytes 1048576 | tf_op jit(solution)/shard_map/all_to_all | solution.py:58
  186.3 15.8 %all-to-all-start.1 = ((bf16[2,2,64,2048]{3,2,1,0:T(8,128)(2,1)}), bf16[2,2,64,2048]{3,2,1,0:T(8,128)(2,1)S(1)}, u32[]{:S(2)}, u32[]{:S(2)}) async-start(bf16[2,2,64,2048]{3,2,1,0:T(8,128)(2,1)} %select_select_fusion), calls=%async_computation.1 | async-start | bytes 2097152 | tf_op jit(solution)/shard_map/all_to_all | solution.py:57
  203.7 10.6 %copy-start.1 = (bf16[512,2048]{1,0:T(8,128)(2,1)S(1)}, bf16[512,2048]{1,0:T(8,128)(2,1)}, u32[]{:S(2)}) copy-start(bf16[512,2048]{1,0:T(8,128)(2,1)} %param.6) | copy-start | bytes 6291460
  203.7 10.6 %copy-start.3 = (bf16[4,64,2048]{2,1,0:T(8,128)(2,1)S(1)}, bf16[4,64,2048]{2,1,0:T(8,128)(2,1)}, u32[]{:S(2)}) copy-start(bf16[4,64,2048]{2,1,0:T(8,128)(2,1)} %gather_fusion.1) | copy-start | bytes 3145732
  214.3 19.9 %copy-start.2 = (bf16[4,64,1024]{2,1,0:T(8,128)(2,1)S(1)}, bf16[4,64,1024]{2,1,0:T(8,128)(2,1)}, u32[]{:S(2)}) copy-start(bf16[4,64,1024]{2,1,0:T(8,128)(2,1)} %gather_fusion.3) | copy-start | bytes 1572868
  214.3 28.6 %collective-permute-start.1 = (f32[512,1024]{1,0:T(8,128)}, f32[512,1024]{1,0:T(8,128)}, u32[]{:S(2)}, u32[]{:S(2)}) collective-permute-start(f32[512,1024]{1,0:T(8,128)} %fusion.15), channel_id=1, source_target_pairs={{0,1},{1,0},{2,3},{3,2},{4,5},{5,4},{6,7},{7,6},{8,9},{9,8},{10,11... | collective-permute-start | bytes 6291464 | tf_op jit(solution)/shard_map/ppermute | solution.py:10
Sparse Core Ops, SparseCore 0:
  8.9 152.3 all-gather.1
where the time goes:
time: 253 us
  waiting for transfers between devices  168 us (66%)
  blocking collectives  24.8 us (10%)
  matrix products  20.1 us (8%)
  between operations  13.6 us (5%)
  local copies, waits for them, and re-layouts  12.6 us (5%)
  starting transfers between devices  7.84 us (3%)
  other arithmetic  5.76 us (2%)
    all_gather x1, waiting for transfers between devices, body(): gathered = lax.all_gather(tokens, 'tp', axis=1, tiled=True)  154 us
    psum x1, blocking collectives, body(): lax.psum(partial_value.reshape(block_count, block_size * rank_width), 'tp')  18.6 us
    dot_general x1, matrix products, body(): their_sums = jnp.dot(borrowed, weight, preferred_element_type=jnp.float32)  10.6 us
    all_to_all x1, waiting for transfers between devices, body(): lax.all_to_all(down_pick, 'ad', split_axis=0, concat_axis=0, tiled=True)  9.75 us
    dot_general x1, matrix products, body(): jnp.dot(own_part, weight, preferred_element_type=jnp.float32) + returned  8.17 us
    all_to_all x1, blocking collectives, body(): lax.all_to_all(requests, 'ad', split_axis=0, concat_axis=0, tiled=True)  6.27 us
  transfers between devices with their start and end apart: 5, of which 3 were waited for; matrix products, arithmetic and copies ran while one was open for 8% of the time, Pallas kernels for 0%

commit v1 on v0

v1 whole, which is shorter than its diff:
```python
import functools

import jax
import jax.numpy as jnp
from jax import lax
from jax.experimental import pallas as pl
from jax.experimental.pallas import tpu as pltpu
from jax.sharding import PartitionSpec as P

MESH = pl.DeviceIdType.MESH
lowrank_scale = 2.0
NT = (((1,), (1,)), ((), ()))


def remote(src, dst, send, recv, device):
    return pltpu.make_async_remote_copy(
        src_ref=src, dst_ref=dst, send_sem=send, recv_sem=recv, device_id=device, device_id_type=MESH
    )


def kernel(
    n, owners, block_count,
    pos, tok, wt, dpick, upick, out,
    g, w, acc, dn, up, part, pre, suf, snd_r, snd_l,
    local, tok_send, tok_recv, w_send, w_recv, a_send, a_recv, sum_send, sum_recv,
):
    z, a, r = lax.axis_index("tp"), lax.axis_index("ad"), lax.axis_index("rep")
    rows, feats = tok.shape
    half = wt.shape[0]
    size = rows // block_count
    per = dpick.shape[0] // owners
    has_left, has_right = z > 0, z < n - 1

    own_tok = pltpu.make_async_copy(tok, g.at[z], local.at[0])
    own_w = pltpu.make_async_copy(wt, w.at[pl.ds(r * half, half)], local.at[1])
    own_dn = pltpu.make_async_copy(dpick.at[pl.ds(a * per, per)], dn.at[pl.ds(a * per, per)], local.at[2])
    own_up = pltpu.make_async_copy(upick.at[pl.ds(a * per, per)], up.at[pl.ds(a * per, per)], local.at[3])
    own_tok.start()

    barrier = pltpu.get_barrier_semaphore()

    @pl.when(has_left)
    def _():
        pl.semaphore_signal(barrier, inc=1, device_id={"tp": z - 1}, device_id_type=MESH)

    @pl.when(has_right)
    def _():
        pl.semaphore_signal(barrier, inc=1, device_id={"tp": z + 1}, device_id_type=MESH)

    pl.semaphore_signal(barrier, inc=1, device_id={"rep": 1 - r}, device_id_type=MESH)
    for d in range(1, owners):
        pl.semaphore_signal(barrier, inc=1, device_id={"ad": lax.rem(a + d, owners)}, device_id_type=MESH)
    own_tok.wait()
    pl.semaphore_wait(
        barrier, owners + jnp.where(has_left, 1, 0) + jnp.where(has_right, 1, 0)
    )

    def piece(shard, c):
        return g.at[shard, pl.ds(pl.multiple_of(c * size, size), size)]

    def to_right(h, c):
        return remote(piece(z - h, c), piece(z - h, c), tok_send.at[0, h, c], tok_recv.at[0, h, c], {"tp": z + 1})

    def to_left(h, c):
        return remote(piece(z + h, c), piece(z + h, c), tok_send.at[1, h, c], tok_recv.at[1, h, c], {"tp": z - 1})

    def from_left(h, c):
        return remote(piece(z - 1 - h, c), piece(z - 1 - h, c), tok_send.at[0, h, c], tok_recv.at[0, h, c], {"tp": z - 1})

    def from_right(h, c):
        return remote(piece(z + 1 + h, c), piece(z + 1 + h, c), tok_send.at[1, h, c], tok_recv.at[1, h, c], {"tp": z + 1})

    def first(c, _):
        @pl.when(has_left)
        def _():
            to_left(0, c).start()

        @pl.when(has_right)
        def _():
            to_right(0, c).start()

        return 0

    lax.fori_loop(0, block_count, first, 0)

    give_w = remote(wt, w.at[pl.ds(r * half, half)], w_send, w_recv, {"rep": 1 - r})
    take_w = remote(wt, w.at[pl.ds((1 - r) * half, half)], w_send, w_recv, {"rep": 1 - r})
    give_w.start()
    own_w.start()
    own_dn.start()
    own_up.start()
    gives, takes = [], []
    for d in range(1, owners):
        to, frm = lax.rem(a + d, owners), lax.rem(a + owners - d, owners)
        for k, (pick, store) in enumerate(((dpick, dn), (upick, up))):
            gives.append(remote(
                pick.at[pl.ds(to * per, per)], store.at[pl.ds(a * per, per)],
                a_send.at[k, d - 1], a_recv.at[k, d - 1], {"ad": to},
            ))
            takes.append(remote(
                pick.at[pl.ds(to * per, per)], store.at[pl.ds(frm * per, per)],
                a_send.at[k, d - 1], a_recv.at[k, d - 1], {"ad": frm},
            ))
            gives[-1].start()

    @pl.when(z == 0)
    def _():
        pre[...] = jnp.zeros_like(pre)

    @pl.when(z == n - 1)
    def _():
        suf[...] = jnp.zeros_like(suf)

    def product(shard, c):
        at = pl.ds(pl.multiple_of(c * size, size), size)
        return jnp.dot(
            g[shard, at, :], w[pl.ds(pl.multiple_of(shard * feats, feats), feats), :],
            preferred_element_type=jnp.float32,
        )

    own_w.wait()
    take_w.wait_recv()

    def own(c, _):
        acc[pl.ds(pl.multiple_of(c * size, size), size), :] = product(z, c)
        return 0

    lax.fori_loop(0, block_count, own, 0)

    own_dn.wait()
    own_up.wait()
    for take in takes:
        take.wait_recv()
    for b in range(block_count):
        part[b] = lax.dot_general(
            dn[pos[b]], g[z, pl.ds(b * size, size), :], NT, preferred_element_type=jnp.float32
        )

    sum_right = remote(snd_r, pre, sum_send.at[0], sum_recv.at[0], {"tp": z + 1})
    sum_left = remote(snd_l, suf, sum_send.at[1], sum_recv.at[1], {"tp": z - 1})

    def hop(h, _):
        def chunk(c, _):
            @pl.when(z - 1 - h >= 0)
            def _():
                from_left(h, c).wait_recv()

                @pl.when(has_right)
                def _():
                    to_right(h + 1, c).start()

            @pl.when(z + 1 + h <= n - 1)
            def _():
                from_right(h, c).wait_recv()

                @pl.when(has_left)
                def _():
                    to_left(h + 1, c).start()

            at = pl.ds(pl.multiple_of(c * size, size), size)

            @pl.when(z - 1 - h >= 0)
            def _():
                acc[at, :] += product(z - 1 - h, c)

            @pl.when(z + 1 + h <= n - 1)
            def _():
                acc[at, :] += product(z + 1 + h, c)

            return 0

        lax.fori_loop(0, block_count, chunk, 0)

        @pl.when((z == h) & has_right)
        def _():
            @pl.when(has_left)
            def _():
                sum_right.wait_recv()

            snd_r[...] = part[...] + pre[...]
            sum_right.start()

        @pl.when((n - 1 - z == h) & has_left)
        def _():
            @pl.when(has_right)
            def _():
                sum_left.wait_recv()

            snd_l[...] = part[...] + suf[...]
            sum_left.start()

        return 0

    lax.fori_loop(0, n - 1, hop, 0)

    @pl.when(z == n - 1)
    def _():
        sum_right.wait_recv()

    @pl.when(z == 0)
    def _():
        sum_left.wait_recv()

    for b in range(block_count):
        at = pl.ds(b * size, size)
        reduced = jnp.transpose(part[b] + pre[b] + suf[b]).astype(jnp.bfloat16)
        lora = jnp.dot(reduced, up[pos[b]], preferred_element_type=jnp.float32)
        out[at, :] = (acc[at, :] + lowrank_scale * lora).astype(jnp.bfloat16)

    def sent(h, _):
        def chunk(c, _):
            @pl.when(has_right & (z - h >= 0))
            def _():
                to_right(h, c).wait_send()

            @pl.when(has_left & (z + h <= n - 1))
            def _():
                to_left(h, c).wait_send()

            return 0

        lax.fori_loop(0, block_count, chunk, 0)
        return 0

    lax.fori_loop(0, n - 1, sent, 0)
    give_w.wait_send()
    for give in gives:
        give.wait_send()

    @pl.when(has_right)
    def _():
        sum_right.wait_send()

    @pl.when(has_left)
    def _():
        sum_left.wait_send()


def body(mesh, tokens, adapter_per_block, placement, weight, lowrank_down_weight, lowrank_up_weight):
    rows, feats = tokens.shape
    block_count = adapter_per_block.shape[0]
    size = rows // block_count
    slots, rank, _ = lowrank_down_weight.shape
    half, columns = weight.shape
    n, owners = mesh.shape["tp"], mesh.shape["ad"]
    per_owner = (block_count + owners - 1) // owners
    table = jnp.arange(placement.shape[0], dtype=jnp.int32)
    store_row = jnp.sum(
        jnp.where(adapter_per_block[:, None] == table[None, :], placement[None, :], 0), axis=1
    )
    owner_of = store_row // slots
    slot_of = store_row % slots
    index = jnp.arange(block_count, dtype=jnp.int32)
    earlier = (owner_of[:, None] == owner_of[None, :]) & (index[None, :] < index[:, None])
    position = owner_of * per_owner + jnp.sum(earlier.astype(jnp.int32), axis=1)
    places = jnp.arange(owners * per_owner, dtype=jnp.int32)
    asks = jnp.sum(jnp.where(position[None, :] == places[:, None], slot_of[None, :], 0), axis=1)
    asked = lax.all_to_all(
        asks.reshape(owners, per_owner), "ad", split_axis=0, concat_axis=0, tiled=True
    ).reshape(-1)
    down_pick = jnp.take(lowrank_down_weight, asked, axis=0, mode="clip")
    up_pick = jnp.take(lowrank_up_weight, asked, axis=0, mode="clip")
    total = owners * per_owner
    bf16, f32 = jnp.bfloat16, jnp.float32
    sums = pltpu.VMEM((block_count, rank, size), f32)
    anyspace = pl.BlockSpec(memory_space=pl.ANY)
    peers = max(owners - 1, 1)
    return pl.pallas_call(
        functools.partial(kernel, n, owners, block_count),
        out_shape=jax.ShapeDtypeStruct((rows, columns), bf16),
        in_specs=[pl.BlockSpec(memory_space=pltpu.SMEM)] + [anyspace] * 4,
        out_specs=pl.BlockSpec(memory_space=pltpu.VMEM),
        scratch_shapes=[
            pltpu.VMEM((n, rows, feats), bf16),
            pltpu.VMEM((2 * half, columns), bf16),
            pltpu.VMEM((rows, columns), f32),
            pltpu.VMEM((total, rank, feats), bf16),
            pltpu.VMEM((total, rank, columns), bf16),
            sums, sums, sums, sums, sums,
            pltpu.SemaphoreType.DMA((4,)),
            pltpu.SemaphoreType.DMA((2, n - 1, block_count)),
            pltpu.SemaphoreType.DMA((2, n - 1, block_count)),
            pltpu.SemaphoreType.DMA,
            pltpu.SemaphoreType.DMA,
            pltpu.SemaphoreType.DMA((2, peers)),
            pltpu.SemaphoreType.DMA((2, peers)),
            pltpu.SemaphoreType.DMA((2,)),
            pltpu.SemaphoreType.DMA((2,)),
        ],
        compiler_params=pltpu.CompilerParams(
            collective_id=0, has_side_effects=True, vmem_limit_bytes=52 * 1024 * 1024
        ),
        cost_estimate=pl.CostEstimate(
            flops=4 * rows * half * columns, bytes_accessed=4 * half * columns, transcendentals=0
        ),
    )(position, tokens, weight, down_pick, up_pick)


def solution(mesh):
    return jax.shard_map(
        functools.partial(body, mesh),
        mesh=mesh,
        in_specs=(
            P(("groups", "ad", "rep"), "tp"),
            P(("groups", "ad", "rep")),
            P(),
            P("rep", "tp"),
            P("ad", None, "tp"),
            P("ad", None, "tp"),
        ),
        out_specs=P(("groups", "ad", "rep"), "tp"),
        check_vma=False,
    )
```

time: 253 us -> 158 us (0.62)
  waiting for transfers between devices: 168 us -> 0 us
  Pallas kernels: 0 us -> 142 us
  matrix products: 20.1 us -> 0 us
  blocking collectives: 24.8 us -> 7.75 us
  between operations: 13.6 us -> 0.02 us
  starting transfers between devices: 7.84 us -> 0 us
  local copies, waits for them, and re-layouts: 12.6 us -> 6.01 us
  other arithmetic: 5.76 us -> 2 us
    all_gather x1 -> x0, waiting for transfers between devices: 154 us -> none  [body(): gathered = lax.all_gather(tokens, 'tp', axis=1, tiled=True)]
    pallas_call x0 -> x1, Pallas kernels: none -> 142 us  [body(): pl.pallas_call(functools.partial(kernel, n, owners, block_count), out_sha...]
    dot_general x4 -> x0, matrix products: 20.1 us -> none  [the longest x1 10.6 us: body(): their_sums = jnp.dot(borrowed, weight, preferred_element_type=jnp.float32)]
    psum x1 -> x0, blocking collectives: 18.6 us -> none  [body(): lax.psum(partial_value.reshape(block_count, block_size * rank_width), 'tp')]
    all_to_all x2 -> x0, waiting for transfers between devices: 13.4 us -> none  [the longest x1 9.75 us: body(): lax.all_to_all(down_pick, 'ad', split_axis=0, concat_axis=0, tiled=True)]
    all_to_all x2 -> x0, starting transfers between devices: 7.78 us -> none  [the longest x1 4.2 us: body(): lax.all_to_all(up_pick, 'ad', split_axis=0, concat_axis=0, tiled=True)]
    dynamic_slice x1 -> x0, local copies, waits for them, and re-layouts: 4.63 us -> none  [body(): lax.dynamic_slice_in_dim(gathered, (1 - core_index) * half_rows, half_row...]
    convert_element_type x1 -> x0, other arithmetic: 3.11 us -> none  [body(): return (base_output + lowrank_scale * lowrank_output).astype(jnp.bfloat16)]
  transfers between devices with their start and end apart: 5 -> 0, of which waited for: 3 -> 0; matrix products, arithmetic and copies ran while one was open for 8% -> 0% of each run, Pallas kernels for 0% -> 0%
where the time goes in v1:
time: 158 us
  Pallas kernels  142 us (90%)
  blocking collectives  7.75 us (5%)
  local copies, waits for them, and re-layouts  6.01 us (4%)
  other arithmetic  2 us (1%)
    pallas_call x1, Pallas kernels, body(): pl.pallas_call(functools.partial(kernel, n, owners, block_count), out_sha...  142 us
    all_to_all x1, blocking collectives, body(): lax.all_to_all(asks.reshape(owners, per_owner), 'ad', split_axis=0, conca...  7.75 us
    gather x1, local copies, waits for them, and re-layouts, body(): down_pick = jnp.take(lowrank_down_weight, asked, axis=0, mode='clip')  3.77 us

profile of v1, /device:TPU:0, one launch (start us, length us, event | category | flops | bytes accessed | tf_op | source)
XLA Modules:
  0.0 158.1 jit_solution(4319635136380903947)
XLA Ops:
  0.0 0.0 copy-start
  0.0 1.0 select_reduce_fusion.1
  1.0 0.2 convert_reduce_fusion
  1.2 0.1 select_reduce_fusion
  1.3 0.1 all_to_all.6
  1.4 7.7 %all_to_all.9 = s32[2,1,2]{2,1,0:T(1,128)S(1)} all-to-all(s32[2,1,2]{2,1,0:T(1,128)S(1)} %bitcast.1), channel_id=1, replica_groups=mesh['groups'=2,'tp'=4,'ad'=2,'rep'=2] {'ad'}, dimensions={0} | all-to-all | bytes 32 | tf_op jit(solution)/shard_map/all_to_all | solution.py:258
  9.2 0.5 broadcast.136
  9.7 0.7 reduce.3
  10.3 0.1 reshape.64
  10.4 0.0 copy-done
  10.4 0.6 gather_fusion.1
  11.0 3.8 %gather_fusion = bf16[4,64,2048]{2,1,0:T(8,128)(2,1)} fusion(bf16[16,64,2048]{2,1,0:T(8,128)(2,1)} %param.10, s32[1024]{0:T(1024)S(1)} %pad_clamp_fusion), kind=kCustom, calls=%fused_computation | custom fusion | bytes 2097168 | tf_op jit(solution)/shard_map/jit(_take)/gather | solution.py:261
  14.8 142.3 %shard_map.64 = bf16[512,1024]{1,0:T(8,128)(2,1)S(1)} custom-call(s32[4]{0:T(128)S(1)} %multiply_add_fusion.pos, bf16[512,2048]{1,0:T(8,128)(2,1)} %tok.1, bf16[4096,1024]{1,0:T(8,128)(2,1)} %wt.1, bf16[4,64,2048]{2,1,0:T(8,128)(2,1)} %gather_fusion, bf16[4,64,1024]{2,1,0:T(8,128)(2,1)S(1)} %gather_fusion.1), custom_call_target="tpu_custom_call" | custom-call | flops 8589934592 | bytes 16777216 | tf_op jit(solution)/shard_map/pallas_call | solution.py:268
  157.1 1.0 copy.10
  (3 shorter events, 0.0 us)
Async XLA Ops:
  0.0 10.4 %copy-start = (bf16[16,64,1024]{2,1,0:T(8,128)(2,1)S(1)}, bf16[16,64,1024]{2,1,0:T(8,128)(2,1)}, u32[]{:S(2)}) copy-start(bf16[16,64,1024]{2,1,0:T(8,128)(2,1)} %param.11) | copy-start | bytes 6291460

commit v2 on v1

--- a/solution.py
+++ b/solution.py
@@ -21,8 +21,9 @@
 def kernel(
     n, owners, block_count,
     pos, tok, wt, dpick, upick, out,
-    g, w, acc, dn, up, part, pre, suf, snd_r, snd_l,
+    g, w, acc, dn, up, part, pre, suf, snd_r, snd_l, wx, far_sum, aid_out, aid_in,
     local, tok_send, tok_recv, w_send, w_recv, a_send, a_recv, sum_send, sum_recv,
+    gv_send, gv_recv, x_send, x_recv, p_send, p_recv, aid_send, aid_recv,
 ):
     z, a, r = lax.axis_index("tp"), lax.axis_index("ad"), lax.axis_index("rep")
     rows, feats = tok.shape
@@ -30,6 +31,12 @@
     size = rows // block_count
     per = dpick.shape[0] // owners
     has_left, has_right = z > 0, z < n - 1
+    mid = n // 2
+    first_end, last_end, by_first, by_last = z == 0, z == n - 1, z == 1, z == n - 2
+    end, helper = first_end | last_end, by_first | by_last
+    end_of, helper_of = jnp.where(by_first, 0, n - 1), jnp.where(first_end, 1, n - 2)
+    giver = (first_end & (r == 1)) | (last_end & (r == 0))
+    sub = half // (2 * owners * block_count)
 
     own_tok = pltpu.make_async_copy(tok, g.at[z], local.at[0])
     own_w = pltpu.make_async_copy(wt, w.at[pl.ds(r * half, half)], local.at[1])
@@ -41,18 +48,20 @@
 
     @pl.when(has_left)
     def _():
-        pl.semaphore_signal(barrier, inc=1, device_id={"tp": z - 1}, device_id_type=MESH)
+        for core in range(2):
+            pl.semaphore_signal(barrier, inc=1, device_id={"tp": z - 1, "rep": core}, device_id_type=MESH)
 
     @pl.when(has_right)
     def _():
-        pl.semaphore_signal(barrier, inc=1, device_id={"tp": z + 1}, device_id_type=MESH)
+        for core in range(2):
+            pl.semaphore_signal(barrier, inc=1, device_id={"tp": z + 1, "rep": core}, device_id_type=MESH)
 
     pl.semaphore_signal(barrier, inc=1, device_id={"rep": 1 - r}, device_id_type=MESH)
     for d in range(1, owners):
         pl.semaphore_signal(barrier, inc=1, device_id={"ad": lax.rem(a + d, owners)}, device_id_type=MESH)
     own_tok.wait()
     pl.semaphore_wait(
-        barrier, owners + jnp.where(has_left, 1, 0) + jnp.where(has_right, 1, 0)
+        barrier, owners + jnp.where(has_left, 2, 0) + jnp.where(has_right, 2, 0)
     )
 
     def piece(shard, c):
@@ -70,12 +79,48 @@
     def from_right(h, c):
         return remote(piece(z + 1 + h, c), piece(z + 1 + h, c), tok_send.at[1, h, c], tok_recv.at[1, h, c], {"tp": z + 1})
 
+    def share(owner, core, j):
+        return pl.ds(pl.multiple_of(((owner * 2 + core) * block_count + j) * sub, sub), sub)
+
+    def give(core, j):
+        at = share(a, core, j)
+        return remote(wt.at[at], wx.at[at], gv_send.at[core, j], gv_recv.at[j], {"tp": helper_of, "rep": core})
+
+    def given(j):
+        at = share(a, r, j)
+        return remote(wt.at[at], wx.at[at], gv_send.at[0, j], gv_recv.at[j], {"tp": end_of})
+
+    def across(d, j):
+        at = wx.at[share(a, r, j)]
+        return remote(at, at, x_send.at[d - 1, j], x_recv.at[d - 1, j], {"ad": lax.rem(a + d, owners)})
+
+    def from_across(d, j):
+        at = wx.at[share(lax.rem(a + owners - d, owners), r, j)]
+        return remote(at, at, x_send.at[d - 1, j], x_recv.at[d - 1, j], {"ad": lax.rem(a + owners - d, owners)})
+
+    def beside(d, core, j):
+        at = wx.at[share(lax.rem(a + owners - d, owners), core, j)]
+        return remote(at, at, p_send.at[d, j], p_recv.at[d, j], {"rep": 1 - r})
+
+    def aid(c, device):
+        at = pl.ds(pl.multiple_of(c * size, size), size)
+        return remote(aid_out.at[at], aid_in.at[at], aid_send.at[c], aid_recv.at[c], {"tp": device})
+
+    @pl.when(giver)
+    def _():
+        def start(j, _):
+            for core in range(2):
+                give(core, j).start()
+            return 0
+
+        lax.fori_loop(0, block_count, start, 0)
+
     def first(c, _):
-        @pl.when(has_left)
+        @pl.when(has_left & jnp.logical_not(last_end))
         def _():
             to_left(0, c).start()
 
-        @pl.when(has_right)
+        @pl.when(has_right & jnp.logical_not(first_end))
         def _():
             to_right(0, c).start()
 
@@ -140,32 +185,91 @@
     sum_left = remote(snd_l, suf, sum_send.at[1], sum_recv.at[1], {"tp": z - 1})
 
     def hop(h, _):
+        hr = h - jnp.where(by_first, 1, 0)
+        hl = h - jnp.where(by_last, 1, 0)
+        left_shard, right_shard = z - 1 - hr, z + 1 + hl
+        takes_left = (hr >= 0) & (left_shard >= 0) & jnp.logical_not(last_end & (left_shard < mid))
+        takes_right = (hl >= 0) & (right_shard <= n - 1) & jnp.logical_not(first_end & (right_shard >= mid))
+
         def chunk(c, _):
-            @pl.when(z - 1 - h >= 0)
-            def _():
-                from_left(h, c).wait_recv()
-
-                @pl.when(has_right)
+            @pl.when(takes_left)
+            def _():
+                from_left(hr, c).wait_recv()
+
+                @pl.when(has_right & jnp.logical_not(by_last & (left_shard < mid)))
                 def _():
-                    to_right(h + 1, c).start()
-
-            @pl.when(z + 1 + h <= n - 1)
-            def _():
-                from_right(h, c).wait_recv()
-
-                @pl.when(has_left)
+                    to_right(hr + 1, c).start()
+
+            @pl.when(takes_right)
+            def _():
+                from_right(hl, c).wait_recv()
+
+                @pl.when(has_left & jnp.logical_not(by_first & (right_shard >= mid)))
                 def _():
-                    to_left(h + 1, c).start()
+                    to_left(hl + 1, c).start()
+
+            @pl.when(end & (h == 0) & (c == block_count - 1))
+            def _():
+                def late(k, _):
+                    @pl.when(first_end)
+                    def _():
+                        to_right(0, k).start()
+
+                    @pl.when(last_end)
+                    def _():
+                        to_left(0, k).start()
+
+                    return 0
+
+                lax.fori_loop(0, block_count, late, 0)
+
+            @pl.when(helper & (h == 0))
+            def _():
+                given(c).wait_recv()
+                for d in range(1, owners):
+                    across(d, c).start()
+                beside(0, r, c).start()
+
+            @pl.when(helper & (h * block_count + c >= 1) & (h * block_count + c <= block_count))
+            def _():
+                for d in range(1, owners):
+                    from_across(d, h * block_count + c - 1).wait_recv()
+                    beside(d, r, h * block_count + c - 1).start()
 
             at = pl.ds(pl.multiple_of(c * size, size), size)
 
-            @pl.when(z - 1 - h >= 0)
-            def _():
-                acc[at, :] += product(z - 1 - h, c)
-
-            @pl.when(z + 1 + h <= n - 1)
-            def _():
-                acc[at, :] += product(z + 1 + h, c)
+            @pl.when(takes_left)
+            def _():
+                acc[at, :] += product(left_shard, c)
+
+            @pl.when(takes_right)
+            def _():
+                acc[at, :] += product(right_shard, c)
+
+            @pl.when(helper & (h == n - 3))
+            def _():
+                @pl.when(c == 0)
+                def _():
+                    def arrived(j, _):
+                        for d in range(owners):
+                            beside(d, 1 - r, j).wait_recv()
+                        return 0
+
+                    lax.fori_loop(0, block_count, arrived, 0)
+
+                base = jnp.where(by_first, mid, 0)
+                far_sum[...] = jnp.zeros_like(far_sum)
+
+                def far(k, _):
+                    far_sum[...] += jnp.dot(
+                        g[base + k, at, :], wx[pl.ds(pl.multiple_of(k * feats, feats), feats), :],
+                        preferred_element_type=jnp.float32,
+                    )
+                    return 0
+
+                lax.fori_loop(0, n - mid, far, 0)
+                aid_out[at, :] = far_sum[...].astype(jnp.bfloat16)
+                aid(c, end_of).start()
 
             return 0
 
@@ -205,15 +309,21 @@
         at = pl.ds(b * size, size)
         reduced = jnp.transpose(part[b] + pre[b] + suf[b]).astype(jnp.bfloat16)
         lora = jnp.dot(reduced, up[pos[b]], preferred_element_type=jnp.float32)
+
+        @pl.when(end)
+        def _():
+            aid(b, helper_of).wait_recv()
+            acc[at, :] += aid_in[at, :].astype(jnp.float32)
+
         out[at, :] = (acc[at, :] + lowrank_scale * lora).astype(jnp.bfloat16)
 
     def sent(h, _):
         def chunk(c, _):
-            @pl.when(has_right & (z - h >= 0))
+            @pl.when(has_right & (z - h >= 0) & jnp.logical_not(by_last & (z - h < mid)))
             def _():
                 to_right(h, c).wait_send()
 
-            @pl.when(has_left & (z + h <= n - 1))
+            @pl.when(has_left & (z + h <= n - 1) & jnp.logical_not(by_first & (z + h >= mid)))
             def _():
                 to_left(h, c).wait_send()
 
@@ -224,8 +334,26 @@
 
     lax.fori_loop(0, n - 1, sent, 0)
     give_w.wait_send()
-    for give in gives:
-        give.wait_send()
+    for gift in gives:
+        gift.wait_send()
+
+    def done(j, _):
+        @pl.when(giver)
+        def _():
+            for core in range(2):
+                give(core, j).wait_send()
+
+        @pl.when(helper)
+        def _():
+            for d in range(1, owners):
+                across(d, j).wait_send()
+            for d in range(owners):
+                beside(d, r, j).wait_send()
+            aid(j, end_of).wait_send()
+
+        return 0
+
+    lax.fori_loop(0, block_count, done, 0)
 
     @pl.when(has_right)
     def _():
@@ -277,6 +405,10 @@
             pltpu.VMEM((total, rank, feats), bf16),
             pltpu.VMEM((total, rank, columns), bf16),
             sums, sums, sums, sums, sums,
+            pltpu.VMEM((half, columns), bf16),
+            pltpu.VMEM((size, columns), f32),
+            pltpu.VMEM((rows, columns), bf16),
+            pltpu.VMEM((rows, columns), bf16),
             pltpu.SemaphoreType.DMA((4,)),
             pltpu.SemaphoreType.DMA((2, n - 1, block_count)),
             pltpu.SemaphoreType.DMA((2, n - 1, block_count)),
@@ -286,9 +418,17 @@
             pltpu.SemaphoreType.DMA((2, peers)),
             pltpu.SemaphoreType.DMA((2,)),
             pltpu.SemaphoreType.DMA((2,)),
+            pltpu.SemaphoreType.DMA((2, block_count)),
+            pltpu.SemaphoreType.DMA((block_count,)),
+            pltpu.SemaphoreType.DMA((peers, block_count)),
+            pltpu.SemaphoreType.DMA((peers, block_count)),
+            pltpu.SemaphoreType.DMA((owners, block_count)),
+            pltpu.SemaphoreType.DMA((owners, block_count)),
+            pltpu.SemaphoreType.DMA((block_count,)),
+            pltpu.SemaphoreType.DMA((block_count,)),
         ],
         compiler_params=pltpu.CompilerParams(
-            collective_id=0, has_side_effects=True, vmem_limit_bytes=52 * 1024 * 1024
+            collective_id=0, has_side_effects=True, vmem_limit_bytes=56 * 1024 * 1024
         ),
         cost_estimate=pl.CostEstimate(
             flops=4 * rows * half * columns, bytes_accessed=4 * half * columns, transcendentals=0

time: 158 us -> 199 us (1.26)
  Pallas kernels: 142 us -> 181 us
  local copies, waits for them, and re-layouts: 6.01 us -> 8.11 us
    pallas_call x1, Pallas kernels: 142 us -> 181 us  [body(): pl.pallas_call(functools.partial(kernel, n, owners, block_count), out_sha...]
where the time goes in v2:
time: 199 us
  Pallas kernels  181 us (91%)
  local copies, waits for them, and re-layouts  8.11 us (4%)
  blocking collectives  7.74 us (4%)
  other arithmetic  1.99 us (1%)
    pallas_call x1, Pallas kernels, body(): pl.pallas_call(functools.partial(kernel, n, owners, block_count), out_sha...  181 us
    all_to_all x1, blocking collectives, body(): lax.all_to_all(asks.reshape(owners, per_owner), 'ad', split_axis=0, conca...  7.74 us

profile of v2, /device:TPU:0, one launch (start us, length us, event | category | flops | bytes accessed | tf_op | source)
XLA Modules:
  0.0 198.9 jit_solution(4482941009565470262)
XLA Ops:
  0.0 0.0 copy-start
  0.0 1.0 select_reduce_fusion.1
  1.0 0.2 convert_reduce_fusion
  1.2 0.0 copy-start.1
  1.2 0.1 select_reduce_fusion
  1.3 0.1 all_to_all.6
  1.4 7.7 %all_to_all.9 = s32[2,1,2]{2,1,0:T(1,128)S(1)} all-to-all(s32[2,1,2]{2,1,0:T(1,128)S(1)} %bitcast.1), channel_id=1, replica_groups=mesh['groups'=2,'tp'=4,'ad'=2,'rep'=2] {'ad'}, dimensions={0} | all-to-all | bytes 32 | tf_op jit(solution)/shard_map/all_to_all | solution.py:386
  9.2 0.5 broadcast.136
  9.7 0.7 reduce.3
  10.3 0.1 reshape.64
  10.4 0.0 copy-done
  10.4 1.4 gather_fusion.1
  11.8 3.8 %gather_fusion = bf16[4,64,2048]{2,1,0:T(8,128)(2,1)} fusion(bf16[16,64,2048]{2,1,0:T(8,128)(2,1)} %param.10, s32[1024]{0:T(1024)S(1)} %pad_clamp_fusion), kind=kCustom, calls=%fused_computation | custom fusion | bytes 2097168 | tf_op jit(solution)/shard_map/jit(_take)/gather | solution.py:389
  15.6 0.0 copy-done.1
  15.6 181.0 %shard_map.64 = bf16[512,1024]{1,0:T(8,128)(2,1)} custom-call(s32[4]{0:T(128)} %copy-done.1, bf16[512,2048]{1,0:T(8,128)(2,1)} %tok.1, bf16[4096,1024]{1,0:T(8,128)(2,1)} %wt.1, bf16[4,64,2048]{2,1,0:T(8,128)(2,1)} %gather_fusion, bf16[4,64,1024]{2,1,0:T(8,128)(2,1)} %gather_fusion.1), custom_call_target="tpu_custom_call" | custom-call | flops 8589934592 | bytes 16777216 | tf_op jit(solution)/shard_map/pallas_call | solution.py:396
  196.7 2.3 %copy.10 = bf16[512,1024]{1,0:T(8,128)(2,1)} copy(bf16[512,1024]{1,0:T(8,128)(2,1)} %shard_map.64) | data formatting | bytes 2097152
  (3 shorter events, 0.0 us)
Async XLA Ops:
  0.0 10.4 %copy-start = (bf16[16,64,1024]{2,1,0:T(8,128)(2,1)S(1)}, bf16[16,64,1024]{2,1,0:T(8,128)(2,1)}, u32[]{:S(2)}) copy-start(bf16[16,64,1024]{2,1,0:T(8,128)(2,1)} %param.11) | copy-start | bytes 6291460
  1.2 14.4 %copy-start.1 = (s32[4]{0:T(128)}, s32[4]{0:T(128)S(1)}, u32[]{:S(2)}) copy-start(s32[4]{0:T(128)S(1)} %multiply_add_fusion.pos) | copy-start | bytes 52

commit v3 on v2

--- a/solution.py
+++ b/solution.py
@@ -191,22 +191,43 @@
         takes_left = (hr >= 0) & (left_shard >= 0) & jnp.logical_not(last_end & (left_shard < mid))
         takes_right = (hl >= 0) & (right_shard <= n - 1) & jnp.logical_not(first_end & (right_shard >= mid))
 
+        def pass_right(c, _=0):
+            from_left(hr, c).wait_recv()
+
+            @pl.when(has_right & jnp.logical_not(by_last & (left_shard < mid)))
+            def _():
+                to_right(hr + 1, c).start()
+
+            return 0
+
+        def pass_left(c, _=0):
+            from_right(hl, c).wait_recv()
+
+            @pl.when(has_left & jnp.logical_not(by_first & (right_shard >= mid)))
+            def _():
+                to_left(hl + 1, c).start()
+
+            return 0
+
         def chunk(c, _):
-            @pl.when(takes_left)
-            def _():
-                from_left(hr, c).wait_recv()
-
-                @pl.when(has_right & jnp.logical_not(by_last & (left_shard < mid)))
-                def _():
-                    to_right(hr + 1, c).start()
-
-            @pl.when(takes_right)
-            def _():
-                from_right(hl, c).wait_recv()
-
-                @pl.when(has_left & jnp.logical_not(by_first & (right_shard >= mid)))
-                def _():
-                    to_left(hl + 1, c).start()
+            low = jnp.where(c == 0, 0, c + 1)
+            high = jnp.where(c + 2 < block_count, c + 2, block_count)
+
+            @pl.when(takes_left & by_first)
+            def _():
+                lax.fori_loop(low, high, pass_right, 0)
+
+            @pl.when(takes_right & by_last)
+            def _():
+                lax.fori_loop(low, high, pass_left, 0)
+
+            @pl.when(takes_left & jnp.logical_not(by_first))
+            def _():
+                pass_right(c)
+
+            @pl.when(takes_right & jnp.logical_not(by_last))
+            def _():
+                pass_left(c)
 
             @pl.when(end & (h == 0) & (c == block_count - 1))
             def _():

time: 199 us -> 141 us (0.71)
  Pallas kernels: 181 us -> 123 us
    pallas_call x1, Pallas kernels: 181 us -> 123 us  [body(): pl.pallas_call(functools.partial(kernel, n, owners, block_count), out_sha...]
where the time goes in v3:
time: 141 us
  Pallas kernels  123 us (87%)
  local copies, waits for them, and re-layouts  8.11 us (6%)
  blocking collectives  7.74 us (5%)
  other arithmetic  1.99 us (1%)
    pallas_call x1, Pallas kernels, body(): pl.pallas_call(functools.partial(kernel, n, owners, block_count), out_sha...  123 us
    all_to_all x1, blocking collectives, body(): lax.all_to_all(asks.reshape(owners, per_owner), 'ad', split_axis=0, conca...  7.74 us
    gather x1, local copies, waits for them, and re-layouts, body(): down_pick = jnp.take(lowrank_down_weight, asked, axis=0, mode='clip')  3.77 us

profile of v3, /device:TPU:0, one launch (start us, length us, event | category | flops | bytes accessed | tf_op | source)
XLA Modules:
  0.0 141.0 jit_solution(1709390690213030596)
XLA Ops:
  0.0 0.0 copy-start
  0.0 1.0 select_reduce_fusion.1
  1.0 0.2 convert_reduce_fusion
  1.2 0.0 copy-start.1
  1.2 0.1 select_reduce_fusion
  1.3 0.1 all_to_all.6
  1.4 7.7 %all_to_all.9 = s32[2,1,2]{2,1,0:T(1,128)S(1)} all-to-all(s32[2,1,2]{2,1,0:T(1,128)S(1)} %bitcast.1), channel_id=1, replica_groups=mesh['groups'=2,'tp'=4,'ad'=2,'rep'=2] {'ad'}, dimensions={0} | all-to-all | bytes 32 | tf_op jit(solution)/shard_map/all_to_all | solution.py:407
  9.2 0.5 broadcast.136
  9.7 0.7 reduce.3
  10.3 0.1 reshape.64
  10.4 0.0 copy-done
  10.4 1.4 gather_fusion.1
  11.8 3.8 %gather_fusion = bf16[4,64,2048]{2,1,0:T(8,128)(2,1)} fusion(bf16[16,64,2048]{2,1,0:T(8,128)(2,1)} %param.10, s32[1024]{0:T(1024)S(1)} %pad_clamp_fusion), kind=kCustom, calls=%fused_computation | custom fusion | bytes 2097168 | tf_op jit(solution)/shard_map/jit(_take)/gather | solution.py:410
  15.6 0.0 copy-done.1
  15.6 123.1 %shard_map.64 = bf16[512,1024]{1,0:T(8,128)(2,1)} custom-call(s32[4]{0:T(128)} %copy-done.1, bf16[512,2048]{1,0:T(8,128)(2,1)} %tok.1, bf16[4096,1024]{1,0:T(8,128)(2,1)} %wt.1, bf16[4,64,2048]{2,1,0:T(8,128)(2,1)} %gather_fusion, bf16[4,64,1024]{2,1,0:T(8,128)(2,1)} %gather_fusion.1), custom_call_target="tpu_custom_call" | custom-call | flops 8589934592 | bytes 16777216 | tf_op jit(solution)/shard_map/pallas_call | solution.py:417
  138.7 2.3 %copy.10 = bf16[512,1024]{1,0:T(8,128)(2,1)} copy(bf16[512,1024]{1,0:T(8,128)(2,1)} %shard_map.64) | data formatting | bytes 2097152
  (3 shorter events, 0.0 us)
Async XLA Ops:
  0.0 10.4 %copy-start = (bf16[16,64,1024]{2,1,0:T(8,128)(2,1)S(1)}, bf16[16,64,1024]{2,1,0:T(8,128)(2,1)}, u32[]{:S(2)}) copy-start(bf16[16,64,1024]{2,1,0:T(8,128)(2,1)} %param.11) | copy-start | bytes 6291460
  1.2 14.4 %copy-start.1 = (s32[4]{0:T(128)}, s32[4]{0:T(128)S(1)}, u32[]{:S(2)}) copy-start(s32[4]{0:T(128)S(1)} %multiply_add_fusion.pos) | copy-start | bytes 52

commit v4 on v3

--- a/solution.py
+++ b/solution.py
@@ -19,13 +19,14 @@
 
 
 def kernel(
-    n, owners, block_count,
+    n, owners, crowd, block_count,
     pos, tok, wt, dpick, upick, out,
     g, w, acc, dn, up, part, pre, suf, snd_r, snd_l, wx, far_sum, aid_out, aid_in,
     local, tok_send, tok_recv, w_send, w_recv, a_send, a_recv, sum_send, sum_recv,
     gv_send, gv_recv, x_send, x_recv, p_send, p_recv, aid_send, aid_recv,
 ):
     z, a, r = lax.axis_index("tp"), lax.axis_index("ad"), lax.axis_index("rep")
+    me = lax.axis_index("groups") * owners + a
     rows, feats = tok.shape
     half = wt.shape[0]
     size = rows // block_count
@@ -36,7 +37,11 @@
     end, helper = first_end | last_end, by_first | by_last
     end_of, helper_of = jnp.where(by_first, 0, n - 1), jnp.where(first_end, 1, n - 2)
     giver = (first_end & (r == 1)) | (last_end & (r == 0))
-    sub = half // (2 * owners * block_count)
+    sub = half // (2 * crowd * block_count)
+
+    def peer(t):
+        return {"groups": t // owners, "ad": lax.rem(t, owners)}
+
 
     own_tok = pltpu.make_async_copy(tok, g.at[z], local.at[0])
     own_w = pltpu.make_async_copy(wt, w.at[pl.ds(r * half, half)], local.at[1])
@@ -57,11 +62,11 @@
             pl.semaphore_signal(barrier, inc=1, device_id={"tp": z + 1, "rep": core}, device_id_type=MESH)
 
     pl.semaphore_signal(barrier, inc=1, device_id={"rep": 1 - r}, device_id_type=MESH)
-    for d in range(1, owners):
-        pl.semaphore_signal(barrier, inc=1, device_id={"ad": lax.rem(a + d, owners)}, device_id_type=MESH)
+    for d in range(1, crowd):
+        pl.semaphore_signal(barrier, inc=1, device_id=peer(lax.rem(me + d, crowd)), device_id_type=MESH)
     own_tok.wait()
     pl.semaphore_wait(
-        barrier, owners + jnp.where(has_left, 2, 0) + jnp.where(has_right, 2, 0)
+        barrier, crowd + jnp.where(has_left, 2, 0) + jnp.where(has_right, 2, 0)
     )
 
     def piece(shard, c):
@@ -83,23 +88,23 @@
         return pl.ds(pl.multiple_of(((owner * 2 + core) * block_count + j) * sub, sub), sub)
 
     def give(core, j):
-        at = share(a, core, j)
+        at = share(me, core, j)
         return remote(wt.at[at], wx.at[at], gv_send.at[core, j], gv_recv.at[j], {"tp": helper_of, "rep": core})
 
     def given(j):
-        at = share(a, r, j)
+        at = share(me, r, j)
         return remote(wt.at[at], wx.at[at], gv_send.at[0, j], gv_recv.at[j], {"tp": end_of})
 
     def across(d, j):
-        at = wx.at[share(a, r, j)]
-        return remote(at, at, x_send.at[d - 1, j], x_recv.at[d - 1, j], {"ad": lax.rem(a + d, owners)})
+        at = wx.at[share(me, r, j)]
+        return remote(at, at, x_send.at[d - 1, j], x_recv.at[d - 1, j], peer(lax.rem(me + d, crowd)))
 
     def from_across(d, j):
-        at = wx.at[share(lax.rem(a + owners - d, owners), r, j)]
-        return remote(at, at, x_send.at[d - 1, j], x_recv.at[d - 1, j], {"ad": lax.rem(a + owners - d, owners)})
+        at = wx.at[share(lax.rem(me + crowd - d, crowd), r, j)]
+        return remote(at, at, x_send.at[d - 1, j], x_recv.at[d - 1, j], peer(lax.rem(me + crowd - d, crowd)))
 
     def beside(d, core, j):
-        at = wx.at[share(lax.rem(a + owners - d, owners), core, j)]
+        at = wx.at[share(lax.rem(me + crowd - d, crowd), core, j)]
         return remote(at, at, p_send.at[d, j], p_recv.at[d, j], {"rep": 1 - r})
 
     def aid(c, device):
@@ -229,7 +234,7 @@
             def _():
                 pass_left(c)
 
-            @pl.when(end & (h == 0) & (c == block_count - 1))
+            @pl.when(end & (h == 0) & (c == (block_count - 1) // 2))
             def _():
                 def late(k, _):
                     @pl.when(first_end)
@@ -247,13 +252,13 @@
             @pl.when(helper & (h == 0))
             def _():
                 given(c).wait_recv()
-                for d in range(1, owners):
+                for d in range(1, crowd):
                     across(d, c).start()
                 beside(0, r, c).start()
 
             @pl.when(helper & (h * block_count + c >= 1) & (h * block_count + c <= block_count))
             def _():
-                for d in range(1, owners):
+                for d in range(1, crowd):
                     from_across(d, h * block_count + c - 1).wait_recv()
                     beside(d, r, h * block_count + c - 1).start()
 
@@ -272,7 +277,7 @@
                 @pl.when(c == 0)
                 def _():
                     def arrived(j, _):
-                        for d in range(owners):
+                        for d in range(crowd):
                             beside(d, 1 - r, j).wait_recv()
                         return 0
 
@@ -366,9 +371,9 @@
 
         @pl.when(helper)
         def _():
-            for d in range(1, owners):
+            for d in range(1, crowd):
                 across(d, j).wait_send()
-            for d in range(owners):
+            for d in range(crowd):
                 beside(d, r, j).wait_send()
             aid(j, end_of).wait_send()
 
@@ -392,6 +397,7 @@
     slots, rank, _ = lowrank_down_weight.shape
     half, columns = weight.shape
     n, owners = mesh.shape["tp"], mesh.shape["ad"]
+    crowd = mesh.shape["groups"] * owners
     per_owner = (block_count + owners - 1) // owners
     table = jnp.arange(placement.shape[0], dtype=jnp.int32)
     store_row = jnp.sum(
@@ -415,7 +421,7 @@
     anyspace = pl.BlockSpec(memory_space=pl.ANY)
     peers = max(owners - 1, 1)
     return pl.pallas_call(
-        functools.partial(kernel, n, owners, block_count),
+        functools.partial(kernel, n, owners, crowd, block_count),
         out_shape=jax.ShapeDtypeStruct((rows, columns), bf16),
         in_specs=[pl.BlockSpec(memory_space=pltpu.SMEM)] + [anyspace] * 4,
         out_specs=pl.BlockSpec(memory_space=pltpu.VMEM),
@@ -441,10 +447,10 @@
             pltpu.SemaphoreType.DMA((2,)),
             pltpu.SemaphoreType.DMA((2, block_count)),
             pltpu.SemaphoreType.DMA((block_count,)),
-            pltpu.SemaphoreType.DMA((peers, block_count)),
-            pltpu.SemaphoreType.DMA((peers, block_count)),
-            pltpu.SemaphoreType.DMA((owners, block_count)),
-            pltpu.SemaphoreType.DMA((owners, block_count)),
+            pltpu.SemaphoreType.DMA((crowd - 1, block_count)),
+            pltpu.SemaphoreType.DMA((crowd - 1, block_count)),
+            pltpu.SemaphoreType.DMA((crowd, block_count)),
+            pltpu.SemaphoreType.DMA((crowd, block_count)),
             pltpu.SemaphoreType.DMA((block_count,)),
             pltpu.SemaphoreType.DMA((block_count,)),
         ],

time: 141 us -> 138 us (0.979)
  Pallas kernels: 123 us -> 120 us
    pallas_call x1, Pallas kernels: 123 us -> 120 us  [body(): pl.pallas_call(functools.partial(kernel, n, owners, crowd, block_count),...]
where the time goes in v4:
time: 138 us
  Pallas kernels  120 us (87%)
  local copies, waits for them, and re-layouts  8.11 us (6%)
  blocking collectives  7.74 us (6%)
  other arithmetic  1.99 us (1%)
    pallas_call x1, Pallas kernels, body(): pl.pallas_call(functools.partial(kernel, n, owners, crowd, block_count),...  120 us
    all_to_all x1, blocking collectives, body(): lax.all_to_all(asks.reshape(owners, per_owner), 'ad', split_axis=0, conca...  7.74 us
    gather x1, local copies, waits for them, and re-layouts, body(): down_pick = jnp.take(lowrank_down_weight, asked, axis=0, mode='clip')  3.77 us

profile of v4, /device:TPU:0, one launch (start us, length us, event | category | flops | bytes accessed | tf_op | source)
XLA Modules:
  0.0 138.0 jit_solution(11732037865214953183)
XLA Ops:
  0.0 0.0 copy-start
  0.0 1.0 select_reduce_fusion.1
  1.0 0.2 convert_reduce_fusion
  1.2 0.0 copy-start.1
  1.2 0.1 select_reduce_fusion
  1.3 0.1 all_to_all.6
  1.4 7.7 %all_to_all.9 = s32[2,1,2]{2,1,0:T(1,128)S(1)} all-to-all(s32[2,1,2]{2,1,0:T(1,128)S(1)} %bitcast.1), channel_id=1, replica_groups=mesh['groups'=2,'tp'=4,'ad'=2,'rep'=2] {'ad'}, dimensions={0} | all-to-all | bytes 32 | tf_op jit(solution)/shard_map/all_to_all | solution.py:413
  9.2 0.5 broadcast.136
  9.7 0.7 reduce.3
  10.3 0.1 reshape.64
  10.4 0.0 copy-done
  10.4 1.4 %gather_fusion.1 = bf16[4,64,1024]{2,1,0:T(8,128)(2,1)} fusion(bf16[16,64,1024]{2,1,0:T(8,128)(2,1)S(1)} %copy-done, s32[1024]{0:T(1024)S(1)} %pad_clamp_fusion), kind=kCustom, calls=%fused_computation.1 | custom fusion | bytes 1048592 | tf_op jit(solution)/shard_map/jit(_take)/gather | solution.py:417
  11.8 3.8 %gather_fusion = bf16[4,64,2048]{2,1,0:T(8,128)(2,1)} fusion(bf16[16,64,2048]{2,1,0:T(8,128)(2,1)} %param.10, s32[1024]{0:T(1024)S(1)} %pad_clamp_fusion), kind=kCustom, calls=%fused_computation | custom fusion | bytes 2097168 | tf_op jit(solution)/shard_map/jit(_take)/gather | solution.py:416
  15.6 0.0 copy-done.1
  15.6 120.2 %shard_map.64 = bf16[512,1024]{1,0:T(8,128)(2,1)} custom-call(s32[4]{0:T(128)} %copy-done.1, bf16[512,2048]{1,0:T(8,128)(2,1)} %tok.1, bf16[4096,1024]{1,0:T(8,128)(2,1)} %wt.1, bf16[4,64,2048]{2,1,0:T(8,128)(2,1)} %gather_fusion, bf16[4,64,1024]{2,1,0:T(8,128)(2,1)} %gather_fusion.1), custom_call_target="tpu_custom_call" | custom-call | flops 8589934592 | bytes 16777216 | tf_op jit(solution)/shard_map/pallas_call | solution.py:423
  135.8 2.3 %copy.10 = bf16[512,1024]{1,0:T(8,128)(2,1)} copy(bf16[512,1024]{1,0:T(8,128)(2,1)} %shard_map.64) | data formatting | bytes 2097152
  (3 shorter events, 0.0 us)
Async XLA Ops:
  0.0 10.4 %copy-start = (bf16[16,64,1024]{2,1,0:T(8,128)(2,1)S(1)}, bf16[16,64,1024]{2,1,0:T(8,128)(2,1)}, u32[]{:S(2)}) copy-start(bf16[16,64,1024]{2,1,0:T(8,128)(2,1)} %param.11) | copy-start | bytes 6291460
  1.2 14.4 %copy-start.1 = (s32[4]{0:T(128)}, s32[4]{0:T(128)S(1)}, u32[]{:S(2)}) copy-start(s32[4]{0:T(128)S(1)} %multiply_add_fusion.pos) | copy-start | bytes 52

commit v5 on v4

--- a/solution.py
+++ b/solution.py
@@ -161,8 +161,12 @@
     def _():
         suf[...] = jnp.zeros_like(suf)
 
-    def product(shard, c):
-        at = pl.ds(pl.multiple_of(c * size, size), size)
+    many = 2 if block_count % 2 == 0 else 1
+
+    def group(c):
+        return pl.ds(pl.multiple_of((c - (many - 1)) * size, size), many * size)
+
+    def product(shard, at):
         return jnp.dot(
             g[shard, at, :], w[pl.ds(pl.multiple_of(shard * feats, feats), feats), :],
             preferred_element_type=jnp.float32,
@@ -172,10 +176,11 @@
     take_w.wait_recv()
 
     def own(c, _):
-        acc[pl.ds(pl.multiple_of(c * size, size), size), :] = product(z, c)
+        at = group(c * many + many - 1)
+        acc[at, :] = product(z, at)
         return 0
 
-    lax.fori_loop(0, block_count, own, 0)
+    lax.fori_loop(0, block_count // many, own, 0)
 
     own_dn.wait()
     own_up.wait()
@@ -262,19 +267,20 @@
                     from_across(d, h * block_count + c - 1).wait_recv()
                     beside(d, r, h * block_count + c - 1).start()
 
-            at = pl.ds(pl.multiple_of(c * size, size), size)
-
-            @pl.when(takes_left)
-            def _():
-                acc[at, :] += product(left_shard, c)
-
-            @pl.when(takes_right)
-            def _():
-                acc[at, :] += product(right_shard, c)
-
-            @pl.when(helper & (h == n - 3))
-            def _():
-                @pl.when(c == 0)
+            at = group(jnp.where(c < many - 1, many - 1, c))
+            whole = lax.rem(c, many) == many - 1
+
+            @pl.when(takes_left & whole)
+            def _():
+                acc[at, :] += product(left_shard, at)
+
+            @pl.when(takes_right & whole)
+            def _():
+                acc[at, :] += product(right_shard, at)
+
+            @pl.when(helper & (h == n - 3) & whole)
+            def _():
+                @pl.when(c == many - 1)
                 def _():
                     def arrived(j, _):
                         for d in range(crowd):
@@ -295,7 +301,8 @@
 
                 lax.fori_loop(0, n - mid, far, 0)
                 aid_out[at, :] = far_sum[...].astype(jnp.bfloat16)
-                aid(c, end_of).start()
+                for k in range(many):
+                    aid(c - (many - 1) + k, end_of).start()
 
             return 0
 
@@ -433,7 +440,7 @@
             pltpu.VMEM((total, rank, columns), bf16),
             sums, sums, sums, sums, sums,
             pltpu.VMEM((half, columns), bf16),
-            pltpu.VMEM((size, columns), f32),
+            pltpu.VMEM((size * (2 if block_count % 2 == 0 else 1), columns), f32),
             pltpu.VMEM((rows, columns), bf16),
             pltpu.VMEM((rows, columns), bf16),
             pltpu.SemaphoreType.DMA((4,)),

time: 138 us -> 146 us (1.058)
  Pallas kernels: 120 us -> 128 us
    pallas_call x1, Pallas kernels: 120 us -> 128 us  [body(): pl.pallas_call(functools.partial(kernel, n, owners, crowd, block_count),...]
where the time goes in v5:
time: 146 us
  Pallas kernels  128 us (88%)
  local copies, waits for them, and re-layouts  8.11 us (6%)
  blocking collectives  7.74 us (5%)
  other arithmetic  1.99 us (1%)
    pallas_call x1, Pallas kernels, body(): pl.pallas_call(functools.partial(kernel, n, owners, crowd, block_count),...  128 us
    all_to_all x1, blocking collectives, body(): lax.all_to_all(asks.reshape(owners, per_owner), 'ad', split_axis=0, conca...  7.74 us
    gather x1, local copies, waits for them, and re-layouts, body(): down_pick = jnp.take(lowrank_down_weight, asked, axis=0, mode='clip')  3.77 us

profile of v5, /device:TPU:0, one launch (start us, length us, event | category | flops | bytes accessed | tf_op | source)
XLA Modules:
  0.0 145.6 jit_solution(10402257816490403192)
XLA Ops:
  0.0 0.0 copy-start
  0.0 1.0 select_reduce_fusion.1
  1.0 0.2 convert_reduce_fusion
  1.2 0.0 copy-start.1
  1.2 0.1 select_reduce_fusion
  1.3 0.1 all_to_all.6
  1.4 7.7 %all_to_all.9 = s32[2,1,2]{2,1,0:T(1,128)S(1)} all-to-all(s32[2,1,2]{2,1,0:T(1,128)S(1)} %bitcast.1), channel_id=1, replica_groups=mesh['groups'=2,'tp'=4,'ad'=2,'rep'=2] {'ad'}, dimensions={0} | all-to-all | bytes 32 | tf_op jit(solution)/shard_map/all_to_all | solution.py:420
  9.2 0.5 broadcast.136
  9.7 0.7 reduce.3
  10.3 0.1 reshape.64
  10.4 0.0 copy-done
  10.4 1.4 gather_fusion.1
  11.8 3.8 %gather_fusion = bf16[4,64,2048]{2,1,0:T(8,128)(2,1)} fusion(bf16[16,64,2048]{2,1,0:T(8,128)(2,1)} %param.10, s32[1024]{0:T(1024)S(1)} %pad_clamp_fusion), kind=kCustom, calls=%fused_computation | custom fusion | bytes 2097168 | tf_op jit(solution)/shard_map/jit(_take)/gather | solution.py:423
  15.6 0.0 copy-done.1
  15.6 127.7 %shard_map.64 = bf16[512,1024]{1,0:T(8,128)(2,1)} custom-call(s32[4]{0:T(128)} %copy-done.1, bf16[512,2048]{1,0:T(8,128)(2,1)} %tok.1, bf16[4096,1024]{1,0:T(8,128)(2,1)} %wt.1, bf16[4,64,2048]{2,1,0:T(8,128)(2,1)} %gather_fusion, bf16[4,64,1024]{2,1,0:T(8,128)(2,1)} %gather_fusion.1), custom_call_target="tpu_custom_call" | custom-call | flops 8589934592 | bytes 16777216 | tf_op jit(solution)/shard_map/pallas_call | solution.py:430
  143.3 2.3 %copy.10 = bf16[512,1024]{1,0:T(8,128)(2,1)} copy(bf16[512,1024]{1,0:T(8,128)(2,1)} %shard_map.64) | data formatting | bytes 2097152
  (3 shorter events, 0.0 us)
Async XLA Ops:
  0.0 10.4 %copy-start = (bf16[16,64,1024]{2,1,0:T(8,128)(2,1)S(1)}, bf16[16,64,1024]{2,1,0:T(8,128)(2,1)}, u32[]{:S(2)}) copy-start(bf16[16,64,1024]{2,1,0:T(8,128)(2,1)} %param.11) | copy-start | bytes 6291460
  1.2 14.4 %copy-start.1 = (s32[4]{0:T(128)}, s32[4]{0:T(128)S(1)}, u32[]{:S(2)}) copy-start(s32[4]{0:T(128)S(1)} %multiply_add_fusion.pos) | copy-start | bytes 52
